TPU v7x, 32 devices: a whole 2x2x4 slice. The times are simulated.
32 devices in a mesh: ctx: 16 (over z, y, x), vid: 2 (over core).
Axes of the slice: x: 2, y: 2, z: 4, core: 2. Of those that a mesh axis runs over, the one named last changes fastest.
Arguments:
- features: bfloat16 [2, 32, 8, 32, 256], P('vid', 'ctx'), may hold values from -6 to 6
- grad_out: bfloat16 [2, 32, 8, 32, 128], P('vid', 'ctx'), may hold values from -6 to 6
- mean_saved: float32 [2, 32], P('vid'), may hold values from -3 to 3
- rstd_saved: float32 [2, 32], P('vid'), may hold values from 0.5 to 2
- latent: float32 [2, 8, 16, 16], P('vid'), may hold values from -6 to 6
- gamma: float32 [256], replicated, may hold values from 0.5 to 1.5
- beta: float32 [256], replicated, may hold values from -3 to 3
- w_scale: float32 [16, 256], replicated, may hold values from -1.5 to 1.5
- b_scale: float32 [256], replicated, may hold values from -3 to 3
- w_shift: float32 [16, 256], replicated, may hold values from -1.5 to 1.5
- b_shift: float32 [256], replicated, may hold values from -3 to 3
- kernel: bfloat16 [6912, 128], replicated, may hold values from -0.078125 to 0.078125
Outputs:
- features_grad: bfloat16 [2, 32, 8, 32, 256], P('vid', 'ctx')
- kernel_grad: float32 [6912, 128], P('ctx', 'vid')
- mod_grads: float32 [2, 16, 256], replicated
- vector_grads: float32 [4, 256], replicated
- latent_grad: float32 [2, 16, 16, 8], P('vid', 'ctx')
All inputs are finite; a program needn't handle non-finite values.
Results may differ from a plain program's by a relative error of at most 0.0029.
Values may be sent and summed in bfloat16 or wider, within the bound.
No kernel may reach another device: no remote copies, remote signals or barrier semaphores. Data moves between devices by JAX's collectives and lax.ppermute only.
A program may use at most 64 MiB of HBM per device.

v0:
```python
import jax
import jax.numpy as jnp
from jax import lax
from jax.sharding import PartitionSpec as P

FR_DEV = 2
H = 8
W = 32
C = 256
CO = 128
G = 32
LP = 16


highest = lax.Precision.HIGHEST


def passed_along(value, axis, steps):
    count = lax.axis_size(axis)
    leading, last = (max(0, -steps), min(count, count - steps))
    return lax.ppermute(value, axis, [(source, source + steps) for source in range(leading, last)])


def swapped(value, axis, apart):
    mask = 2**apart
    pairs = [(source, source ^ mask) for source in range(lax.axis_size(axis))]
    return lax.ppermute(value, axis, pairs)


def spread_frame(table):
    grid = table.reshape(H // 4, W // 4, C)
    wide = jnp.broadcast_to(grid[:, None, :, None, :], (H // 4, 4, W // 4, 4, C))
    return wide.reshape(1, H, W, C)


def pool_frames(field):
    frames = field.shape[0]
    return field.reshape(frames, H // 4, 4, W // 4, 4, C).sum(axis=(0, 2, 4)).reshape(LP, C)


def transpose_conv(grad_pad, tap_weights, frames):
    total = jnp.zeros((frames * H * W, C), jnp.float32)
    for frame_tap in range(3):
        for row_tap in range(3):
            for col_tap in range(3):
                source = grad_pad[
                    2 - frame_tap : 2 - frame_tap + frames,
                    2 - row_tap : 2 - row_tap + H,
                    2 - col_tap : 2 - col_tap + W,
                ].reshape(frames * H * W, CO)
                total = total + lax.dot_general(
                    source,
                    tap_weights[frame_tap, row_tap, col_tap],
                    (((1,), (1,)), ((), ())),
                    preferred_element_type=jnp.float32,
                )
    return total.reshape(frames, H, W, C)


def local(
    features,
    grad_out,
    mean_saved,
    rstd_saved,
    latent,
    gamma,
    beta,
    w_scale,
    b_scale,
    w_shift,
    b_shift,
    kernel,
):
    device = lax.axis_index("ctx")
    frames_in = features[0]
    grads_in = grad_out[0]
    mean_chan = jnp.broadcast_to(mean_saved[0][:, None], (G, C // G)).reshape(C)
    rstd_chan = jnp.broadcast_to(rstd_saved[0][:, None], (G, C // G)).reshape(C)
    normed = (frames_in.astype(jnp.float32) - mean_chan) * rstd_chan
    latent_frame = lax.dynamic_index_in_dim(latent[0], device // 2, 0, keepdims=False)
    scale_tab = jnp.einsum("zp,zc->pc", latent_frame, w_scale, precision=highest) + b_scale
    shift_tab = jnp.einsum("zp,zc->pc", latent_frame, w_shift, precision=highest) + b_shift
    scale_map = spread_frame(scale_tab)
    shift_map = spread_frame(shift_tab)
    base_map = normed * gamma + beta
    modulated = base_map * scale_map + shift_map
    squashed = jax.nn.sigmoid(modulated)
    activated = (modulated * squashed).astype(jnp.bfloat16)
    before = passed_along(activated, "ctx", 1)
    leading = jnp.broadcast_to(activated[:1], before.shape)
    before = jnp.where(device == 0, leading, before)
    padded = jnp.pad(jnp.concatenate([before, activated], 0), ((0, 0), (1, 1), (1, 1), (0, 0)))
    tap_weights = kernel.reshape(3, 3, 3, C, CO)
    grads_rows = grads_in.reshape(FR_DEV * H * W, CO)
    pieces = []
    for frame_tap in range(3):
        for row_tap in range(3):
            for col_tap in range(3):
                window = padded[
                    frame_tap : frame_tap + FR_DEV, row_tap : row_tap + H, col_tap : col_tap + W
                ].reshape(FR_DEV * H * W, C)
                pieces.append(
                    lax.dot_general(
                        window,
                        grads_rows,
                        (((0,), (0,)), ((), ())),
                        preferred_element_type=jnp.float32,
                    )
                )
    kernel_term = jnp.stack(pieces).reshape(27 * C, CO)
    beyond = passed_along(grads_in, "ctx", -1)
    grad_pad = jnp.pad(jnp.concatenate([grads_in, beyond], 0), ((2, 0), (1, 1), (1, 1), (0, 0)))
    extended = transpose_conv(grad_pad, tap_weights, FR_DEV + 2)
    act_grad = extended[2:]
    virtual = jnp.where(device == 0, extended[0] + extended[1], 0.0)
    act_grad = act_grad.at[0].add(virtual)
    pre_grad = act_grad * squashed * (1.0 + modulated * (1.0 - squashed))
    features_grad = (pre_grad * scale_map * gamma * rstd_chan).astype(jnp.bfloat16)
    scale_pool = pool_frames(pre_grad * base_map)
    shift_pool = pool_frames(pre_grad)
    mod_part = jnp.stack(
        [
            jnp.einsum("zp,pc->zc", latent_frame, scale_pool, precision=highest),
            jnp.einsum("zp,pc->zc", latent_frame, shift_pool, precision=highest),
        ]
    )
    vec_part = jnp.stack(
        [
            jnp.sum(pre_grad * scale_map * normed, axis=(0, 1, 2)),
            jnp.sum(pre_grad * scale_map, axis=(0, 1, 2)),
            jnp.sum(scale_pool, axis=0),
            jnp.sum(shift_pool, axis=0),
        ]
    )
    latent_sum = jnp.einsum("zc,pc->zp", w_scale, scale_pool, precision=highest) + jnp.einsum(
        "zc,pc->zp", w_shift, shift_pool, precision=highest
    )
    half_len = LP // 2
    parity = device % 2
    own_half = lax.dynamic_slice_in_dim(latent_sum, parity * half_len, half_len, 1)
    far_half = lax.dynamic_slice_in_dim(latent_sum, (1 - parity) * half_len, half_len, 1)
    received = swapped(far_half, "ctx", 0)
    latent_grad = (own_half + received)[None, None]
    mod_grads, vector_grads = lax.psum((mod_part, vec_part), ("ctx", "vid"))
    kernel_part = lax.psum_scatter(kernel_term, "vid", scatter_dimension=1, tiled=True)
    kernel_grad = lax.psum_scatter(kernel_part, "ctx", scatter_dimension=0, tiled=True)
    return (features_grad[None], kernel_grad, mod_grads, vector_grads, latent_grad)


def solution(mesh):
    placed = (
        P("vid", "ctx", None, None, None),
        P("vid", "ctx", None, None, None),
        P("vid", None),
        P("vid", None),
        P("vid", None, None, None),
        P(),
        P(),
        P(),
        P(),
        P(),
        P(),
        P(),
    )
    return jax.shard_map(
        local,
        mesh=mesh,
        in_specs=placed,
        out_specs=(
            P("vid", "ctx", None, None, None),
            P("ctx", "vid"),
            P(),
            P(),
            P("vid", "ctx", None, None),
        ),
        check_vma=False,
    )
```

profile of v0, /device:TPU:0, one launch (start us, length us, event | category | flops | bytes accessed | tf_op | source)
XLA Modules:
  0.0 215.7 jit_solution(3597291985840509583)
XLA Ops:
  7.2 1.3 collective-permute-start
  8.6 0.9 fusion.28
  9.5 0.7 broadcast_in_dim.52
  10.3 0.7 broadcast_in_dim.54
  11.3 0.9 fusion.29
  12.3 3.4 %collective-permute-done = bf16[2,8,32,128]{3,2,1,0:T(8,128)(2,1)S(1)} collective-permute-done((bf16[2,8,32,128]{3,2,1,0:T(8,128)(2,1)}, bf16[2,8,32,128]{3,2,1,0:T(8,128)(2,1)S(1)}, u32[]{:S(2)}, u32[]{:S(2)}) %collective-permute-start) | collective-permute-done | bytes 131104 | tf_op jit(solution)/shard_map/ppermute | solution.py:21
  15.8 0.9 pad_maximum_fusion.1
  16.7 0.3 pad_slice_fusion.1
  17.1 0.9 pad_slice_fusion
  18.5 0.3 fusion.44
  18.8 0.3 convolution_add_fusion.24
  20.0 0.3 convolution_add_fusion.20
  21.7 0.3 convolution_add_fusion.14
  22.0 0.3 convolution_add_fusion.13
  23.5 0.3 convolution_add_fusion.8
  23.8 0.3 convolution_add_fusion.7
  25.3 0.3 convolution_add_fusion.2
  26.6 0.5 fusion.42
  27.1 4.7 %collective-permute-start.1 = (bf16[2,8,32,256]{3,2,1,0:T(8,128)(2,1)S(1)}, bf16[2,8,32,256]{3,2,1,0:T(8,128)(2,1)S(1)}, u32[]{:S(2)}, u32[]{:S(2)}) collective-permute-start(bf16[2,8,32,256]{3,2,1,0:T(8,128)(2,1)S(1)} %get-tuple-element.26), channel_id=1, source_target_pairs={{0,2},{2,4},{4,6},{6,8},{8,10},{10,12},{12,14},{14,16},{16,18},{18... | collective-permute-start | bytes 786440 | tf_op jit(solution)/shard_map/ppermute | solution.py:21
  31.8 4.5 %collective-permute-done.1 = bf16[2,8,32,256]{3,2,1,0:T(8,128)(2,1)S(1)} collective-permute-done((bf16[2,8,32,256]{3,2,1,0:T(8,128)(2,1)S(1)}, bf16[2,8,32,256]{3,2,1,0:T(8,128)(2,1)S(1)}, u32[]{:S(2)}, u32[]{:S(2)}) %collective-permute-start.1) | collective-permute-done | bytes 262176 | tf_op jit(solution)/shard_map/ppermute | solution.py:21
  36.7 0.9 pad_slice_fusion.26
  45.2 1.8 copy-done.2
  47.0 5.2 %copy.21 = f32[6912,128]{0,1:T(8,128)} copy(f32[6912,128]{1,0:T(8,128)} %bitcast.423) | data formatting | bytes 7077888 | tf_op jit(solution)/shard_map/reshape | solution.py:110
  52.2 14.1 %reduce-scatter.5.cloned.1.call-done = f32[6912,64]{0,1:T(8,128)} async-done(((f32[6912,128]{0,1:T(8,128)}), f32[6912,64]{0,1:T(8,128)}) %reduce-scatter.5.cloned.1.call-update) | async-done | bytes 1769488 | tf_op jit(solution)/shard_map/reduce_scatter | solution.py:145
  66.3 3.5 %copy.24 = f32[6912,64]{1,0:T(8,128)} copy(f32[6912,64]{0,1:T(8,128)} %reduce-scatter.5.cloned.1.call-done) | data formatting | bytes 3538944
  70.1 0.4 copy-done.6
  70.8 1.8 collective-permute-start.2
  72.8 0.8 fusion.38
  73.6 40.7 %all-reduce.2 = (f32[2,16,256]{2,1,0:T(8,128)}, f32[4,256]{1,0:T(4,128)}) all-reduce(f32[2,16,256]{2,1,0:T(8,128)S(1)} %pad_maximum_fusion.2, f32[4,256]{1,0:T(4,128)S(1)} %pad_maximum_fusion.3), channel_id=1, replica_groups=mesh['ctx'=16,'vid'=2] {'ctx','vid'}, use_global_device_ids=true, to_apply=%region_6.7 | all-reduce | flops 9216 | bytes 73728 | tf_op jit(solution)/shard_map/psum | solution.py:144
  114.3 0.6 fusion.59
  114.9 92.2 %reduce-scatter.7.cloned.1.call-done = f32[432,64]{1,0:T(8,128)} async-done(((f32[6912,64]{1,0:T(8,128)}), f32[432,64]{1,0:T(8,128)}) %reduce-scatter.7.cloned.1.call-update) | async-done | bytes 110608
  207.2 1.7 copy.25
  (92 shorter events, 15.1 us)
Async XLA Ops:
  7.2 1.4 copy-start
  7.2 59.1 %reduce-scatter.5.cloned.1.call-start = ((), (), s32[]{:S(2)}) async-start(), calls=%async_computation.2 | async-start | bytes 5308416 | tf_op jit(solution)/shard_map/reduce_scatter | solution.py:145
  7.2 8.5 %collective-permute-start = (bf16[2,8,32,128]{3,2,1,0:T(8,128)(2,1)}, bf16[2,8,32,128]{3,2,1,0:T(8,128)(2,1)S(1)}, u32[]{:S(2)}, u32[]{:S(2)}) collective-permute-start(bf16[2,8,32,128]{3,2,1,0:T(8,128)(2,1)} %bitcast.391), channel_id=1, source_target_pairs={{2,0},{4,2},{6,4},{8,6},{10,8},{12,10},{14,12},{16,14},{18,16},{20... | collective-permute-start | bytes 393224 | tf_op jit(solution)/shard_map/ppermute | solution.py:21
  16.7 1.5 copy-start.3
  25.6 1.0 copy-start.4
  25.6 0.9 copy-start.7
  25.6 0.9 copy-start.8
  27.1 9.2 %collective-permute-start.1 = (bf16[2,8,32,256]{3,2,1,0:T(8,128)(2,1)S(1)}, bf16[2,8,32,256]{3,2,1,0:T(8,128)(2,1)S(1)}, u32[]{:S(2)}, u32[]{:S(2)}) collective-permute-start(bf16[2,8,32,256]{3,2,1,0:T(8,128)(2,1)S(1)} %get-tuple-element.26), channel_id=1, source_target_pairs={{0,2},{2,4},{4,6},{6,8},{8,10},{10,12},{12,14},{14,16},{16,18},{18... | collective-permute-start | bytes 786440 | tf_op jit(solution)/shard_map/ppermute | solution.py:21
  36.4 1.2 copy-start.1
  45.1 1.8 copy-start.2
  52.2 155.0 %reduce-scatter.7.cloned.1.call-start = ((), (), s32[]{:S(2)}) async-start(), calls=%async_computation.3 | async-start | bytes 3760128
  69.8 0.7 copy-start.6
  69.8 0.8 copy-start.5
  70.8 43.6 %collective-permute-start.2 = (f32[16,8]{0,1:T(8,128)S(1)}, f32[16,8]{0,1:T(8,128)S(1)}, u32[]{:S(2)}, u32[]{:S(2)}) collective-permute-start(f32[16,8]{0,1:T(8,128)S(1)} %dynamic-slice_bitcast_fusion), channel_id=1, source_target_pairs={{0,2},{2,0},{4,6},{6,4},{8,10},{10,8},{12,14},{14,12},{16,18},{18,... | collective-permute-start | bytes 1544 | tf_op jit(solution)/shard_map/ppermute | solution.py:27
Sparse Core Ops, SparseCore 0:
  52.3 13.9 reduce-scatter.4
  72.2 134.9 reduce-scatter.6
where the time goes:
time: 216 us
  waiting for transfers between devices  114 us (53%)
  blocking collectives  40.7 us (19%)
  local copies, waits for them, and re-layouts  17.5 us (8%)
  matrix products  17.5 us (8%)
  between operations  14.8 us (7%)
  starting transfers between devices  7.88 us (4%)
  other arithmetic  3.09 us (1%)
    unnamed x3, waiting for transfers between devices  92.3 us
    psum x1, blocking collectives, local(): mod_grads, vector_grads = lax.psum((mod_part, vec_part), ('ctx', 'vid'))  40.7 us
    reduce_scatter x1, waiting for transfers between devices, local(): lax.psum_scatter(kernel_term, 'vid', scatter_dimension=1, tiled=True)  14.1 us
    ppermute x2, waiting for transfers between devices, passed_along(): lax.ppermute(value, axis, [(source, source + steps) for source in range(l...  7.9 us
    dot_general x27, matrix products, transpose_conv(): lax.dot_general(source, tap_weights[frame_tap, row_tap, col_tap], (((1,),...  7.86 us
    unnamed x20, local copies, waits for them, and re-layouts  7.76 us
    dot_general x27, matrix products, local(): lax.dot_general(window, grads_rows, (((0,), (0,)), ((), ())), preferred_e...  7.29 us
    ppermute x2, starting transfers between devices, passed_along(): lax.ppermute(value, axis, [(source, source + steps) for source in range(l...  6.04 us
  transfers between devices with their start and end apart: 5, of which 4 were waited for; matrix products, arithmetic and copies ran while one was open for 3% of the time, Pallas kernels for 0%

commit v1 on v0

--- a/solution.py
+++ b/solution.py
@@ -1,3 +1,5 @@
+import math
+
 import jax
 import jax.numpy as jnp
 from jax import lax
@@ -10,6 +12,7 @@
 CO = 128
 G = 32
 LP = 16
+NEAR = 4
 
 
 highest = lax.Precision.HIGHEST
@@ -25,6 +28,43 @@
     mask = 2**apart
     pairs = [(source, source ^ mask) for source in range(lax.axis_size(axis))]
     return lax.ppermute(value, axis, pairs)
+
+
+def rotated(value, turn, axis):
+    count = lax.axis_size(axis)
+    return lax.ppermute(value, axis, [(source, (source + turn) % count) for source in range(count)])
+
+
+def near_groups(count):
+    near = math.gcd(count, NEAR)
+    base = [source - source % near for source in range(count)]
+    return near, lambda source, turn: base[source] + (source + turn) % near
+
+
+def far_groups(count):
+    near = math.gcd(count, NEAR)
+    return count // near, lambda source, turn: (source + turn * near) % count
+
+
+def exchange_sum(value, axis, groups):
+    count = lax.axis_size(axis)
+    size, target = groups(count)
+    total = value
+    for turn in range(1, size):
+        total = total + lax.ppermute(value, axis, [(s, target(s, turn)) for s in range(count)])
+    return total
+
+
+def scatter_sum(blocks, place, groups):
+    count = lax.axis_size("ctx")
+    size, target = groups(count)
+    total = lax.dynamic_index_in_dim(blocks, place, 0, keepdims=False)
+    narrow = blocks.astype(jnp.bfloat16)
+    for turn in range(1, size):
+        sent = lax.dynamic_index_in_dim(narrow, (place + turn) % size, 0, keepdims=False)
+        got = lax.ppermute(sent, "ctx", [(s, target(s, turn)) for s in range(count)])
+        total = total + got.astype(jnp.float32)
+    return total
 
 
 def spread_frame(table):
@@ -141,9 +181,32 @@
     far_half = lax.dynamic_slice_in_dim(latent_sum, (1 - parity) * half_len, half_len, 1)
     received = swapped(far_half, "ctx", 0)
     latent_grad = (own_half + received)[None, None]
-    mod_grads, vector_grads = lax.psum((mod_part, vec_part), ("ctx", "vid"))
-    kernel_part = lax.psum_scatter(kernel_term, "vid", scatter_dimension=1, tiled=True)
-    kernel_grad = lax.psum_scatter(kernel_part, "ctx", scatter_dimension=0, tiled=True)
+    small = jnp.concatenate([mod_part.reshape(-1, C), vec_part], 0)
+    small = small + rotated(small, 1, "vid")
+    small = exchange_sum(small, "ctx", near_groups)
+    small = exchange_sum(small, "ctx", far_groups)
+    mod_grads = small[: 2 * latent.shape[2]].reshape(2, latent.shape[2], C)
+    vector_grads = small[2 * latent.shape[2] :]
+
+    videos = lax.axis_size("vid")
+    count = lax.axis_size("ctx")
+    near = math.gcd(count, NEAR)
+    far = count // near
+    rows, cols = 27 * C // count, CO // videos
+    piece = -(-rows // (16 * videos)) * 16
+    blocks = kernel_term.reshape(count, rows, videos, cols)
+    blocks = jnp.pad(blocks, ((0, 0), (0, videos * piece - rows), (0, 0), (0, 0)))
+    blocks = blocks.reshape(count, videos, piece, videos, cols)
+    blocks = blocks.transpose(3, 0, 2, 1, 4).reshape(videos, count, piece, CO)
+    here = lax.axis_index("vid")
+    total = lax.dynamic_index_in_dim(blocks, here, 0, keepdims=False)
+    for turn in range(1, videos):
+        sent = lax.dynamic_index_in_dim(blocks, (here + turn) % videos, 0, keepdims=False)
+        total = total + rotated(sent, turn, "vid")
+    blocks = total.reshape(far, near, piece, CO).transpose(1, 0, 2, 3)
+    total = scatter_sum(blocks, device % near, near_groups)
+    total = scatter_sum(total, device // near, far_groups)
+    kernel_grad = total.reshape(piece, videos, cols).transpose(1, 0, 2).reshape(videos * piece, cols)[:rows]
     return (features_grad[None], kernel_grad, mod_grads, vector_grads, latent_grad)
 
 

time: 216 us -> 130 us (0.60)
  waiting for transfers between devices: 114 us -> 13.8 us
  blocking collectives: 40.7 us -> 0 us
  local copies, waits for them, and re-layouts: 17.5 us -> 43.3 us
  starting transfers between devices: 7.88 us -> 28.8 us
  matrix products: 17.5 us -> 35.2 us
  between operations: 14.8 us -> 1.21 us
  other arithmetic: 3.09 us -> 6.45 us
    unnamed x3 -> x0, waiting for transfers between devices: 92.3 us -> none
    psum x1 -> x0, blocking collectives: 40.7 us -> none  [local(): mod_grads, vector_grads = lax.psum((mod_part, vec_part), ('ctx', 'vid'))]
    ppermute x0 -> x14, starting transfers between devices: none -> 20.1 us  [the longest x6 10.7 us: exchange_sum(): lax.ppermute(value, axis, [(s, target(s, turn)) for s in range(count)])]
    dot_general x27, matrix products: 7.29 us -> 25 us  [local(): lax.dot_general(window, grads_rows, (((0,), (0,)), ((), ())), preferred_e...]
    reduce_scatter x1 -> x0, waiting for transfers between devices: 14.1 us -> none  [local(): lax.psum_scatter(kernel_term, 'vid', scatter_dimension=1, tiled=True)]
    another operation x0 -> x2, local copies, waits for them, and re-layouts: none -> 12.6 us  [the longest x1 7.05 us: local(): blocks = kernel_term.reshape(count, rows, videos, cols)]
    unnamed x20 -> x16, local copies, waits for them, and re-layouts: 7.76 us -> 0.41 us
    reshape x1 -> x3, local copies, waits for them, and re-layouts: 5.18 us -> 12.1 us  [the longest x2 11.3 us: local(): blocks = blocks.reshape(count, videos, piece, videos, cols)]
  transfers between devices with their start and end apart: 5 -> 17, of which waited for: 4 -> 10; matrix products, arithmetic and copies ran while one was open for 3% -> 10% of each run, Pallas kernels for 0% -> 0%
where the time goes in v1:
time: 130 us; the launch traced here: 129 us
  local copies, waits for them, and re-layouts  43.3 us (33%)
  matrix products  35.2 us (27%)
  starting transfers between devices  28.8 us (22%)
  waiting for transfers between devices  13.8 us (11%)
  other arithmetic  6.45 us (5%)
    dot_general x27, matrix products, local(): lax.dot_general(window, grads_rows, (((0,), (0,)), ((), ())), preferred_e...  25 us
    reshape x2, local copies, waits for them, and re-layouts, local(): blocks = blocks.reshape(count, videos, piece, videos, cols)  11.3 us
    ppermute x6, starting transfers between devices, exchange_sum(): lax.ppermute(value, axis, [(s, target(s, turn)) for s in range(count)])  10.7 us
    ppermute x6, starting transfers between devices, scatter_sum(): lax.ppermute(sent, 'ctx', [(s, target(s, turn)) for s in range(count)])  9.07 us
    dot_general x27, matrix products, transpose_conv(): lax.dot_general(source, tap_weights[frame_tap, row_tap, col_tap], (((1,),...  7.88 us
    ppermute x2, waiting for transfers between devices, passed_along(): lax.ppermute(value, axis, [(source, source + steps) for source in range(l...  7.87 us
    another operation x1, local copies, waits for them, and re-layouts, local(): blocks = kernel_term.reshape(count, rows, videos, cols)  7.05 us
    ppermute x2, starting transfers between devices, passed_along(): lax.ppermute(value, axis, [(source, source + steps) for source in range(l...  6.17 us
  transfers between devices with their start and end apart: 17, of which 10 were waited for; matrix products, arithmetic and copies ran while one was open for 10% of the time, Pallas kernels for 0%

profile of v1, /device:TPU:0, one launch (start us, length us, event | category | flops | bytes accessed | tf_op | source)
XLA Modules:
  0.0 128.8 jit_solution(10432820782056372030)
XLA Ops:
  0.6 1.4 %collective-permute-start = (bf16[2,8,32,128]{3,2,1,0:T(8,128)(2,1)}, bf16[2,8,32,128]{3,2,1,0:T(8,128)(2,1)S(1)}, u32[]{:S(2)}, u32[]{:S(2)}) collective-permute-start(bf16[2,8,32,128]{3,2,1,0:T(8,128)(2,1)} %bitcast.435), channel_id=1, source_target_pairs={{2,0},{4,2},{6,4},{8,6},{10,8},{12,10},{14,12},{16,14},{18,16},{20... | collective-permute-start | bytes 393224 | tf_op jit(solution)/shard_map/ppermute | solution.py:24
  5.9 3.4 %collective-permute-done = bf16[2,8,32,128]{3,2,1,0:T(8,128)(2,1)S(1)} collective-permute-done((bf16[2,8,32,128]{3,2,1,0:T(8,128)(2,1)}, bf16[2,8,32,128]{3,2,1,0:T(8,128)(2,1)S(1)}, u32[]{:S(2)}, u32[]{:S(2)}) %collective-permute-start) | collective-permute-done | bytes 131104 | tf_op jit(solution)/shard_map/ppermute | solution.py:24
  10.6 1.0 pad_slice_fusion
  20.6 4.7 %collective-permute-start.1 = (bf16[2,8,32,256]{3,2,1,0:T(8,128)(2,1)S(1)}, bf16[2,8,32,256]{3,2,1,0:T(8,128)(2,1)S(1)}, u32[]{:S(2)}, u32[]{:S(2)}) collective-permute-start(bf16[2,8,32,256]{3,2,1,0:T(8,128)(2,1)S(1)} %get-tuple-element.31), channel_id=1, source_target_pairs={{0,2},{2,4},{4,6},{6,8},{8,10},{10,12},{12,14},{14,16},{16,18},{18... | collective-permute-start | bytes 786440 | tf_op jit(solution)/shard_map/ppermute | solution.py:24
  25.4 4.5 %collective-permute-done.1 = bf16[2,8,32,256]{3,2,1,0:T(8,128)(2,1)S(1)} collective-permute-done((bf16[2,8,32,256]{3,2,1,0:T(8,128)(2,1)S(1)}, bf16[2,8,32,256]{3,2,1,0:T(8,128)(2,1)S(1)}, u32[]{:S(2)}, u32[]{:S(2)}) %collective-permute-start.1) | collective-permute-done | bytes 262176 | tf_op jit(solution)/shard_map/ppermute | solution.py:24
  32.1 0.9 fusion.26
  39.5 0.9 fusion.18
  40.4 0.9 fusion.17
  41.3 0.9 fusion.16
  42.3 0.9 fusion.15
  43.2 1.0 fusion.14
  48.8 0.9 fusion.8
  51.5 0.9 fusion.5
  56.2 5.5 %copy.57 = f32[27,256,128]{1,0,2:T(8,128)} copy(f32[27,256,128]{2,1,0:T(8,128)} %fusion.1) | data formatting | bytes 7077888 | tf_op jit(solution)/shard_map/stack | solution.py:150
  61.7 7.0 %reshape_reshape.3 = f32[16,432,2,64]{1,0,3,2:T(8,128)} reshape(f32[27,256,128]{1,0,2:T(8,128)} %copy.57) | data formatting | bytes 7077888 | tf_op jit(solution)/shard_map/reshape;reshape | solution.py:197
  68.7 5.0 %pad.16 = f32[16,448,2,64]{1,0,3,2:T(8,128)} pad(f32[16,432,2,64]{1,0,3,2:T(8,128)} %reshape_reshape.3, f32[]{:T(128)} %constant.144.clone.1), padding=0_0x0_16x0_0x0_0 | pad | bytes 7208964 | tf_op jit(solution)/shard_map/jit(_pad)/pad | solution.py:198
  73.7 6.7 %reshape.421 = f32[16,2,224,2,64]{2,1,0,4,3:T(2,128)} reshape(f32[16,448,2,64]{1,0,3,2:T(8,128)} %pad.16) | data formatting | bytes 7340032 | tf_op jit(solution)/shard_map/reshape | solution.py:199
  80.4 4.6 %copy.58 = f32[16,2,224,2,64]{2,4,1,0,3:T(8,128)S(1)} copy(f32[16,2,224,2,64]{2,1,0,4,3:T(2,128)} %reshape.421) | data formatting | bytes 7340032 | tf_op jit(solution)/shard_map/reshape | solution.py:199
  85.0 1.8 %constant_dynamic-slice_fusion.1 = (f32[1,16,224,128]{2,3,1,0:T(8,128)S(1)}, f32[1,16,224,128]{2,3,1,0:T(8,128)}) fusion(f32[2,16,224,128]{2,3,1,0:T(8,128)S(1)} %bitcast.464, s32[]{:T(128)S(6)} %select_n.119, s32[]{:T(128)S(6)} %select_n.121), kind=kLoop, calls=%fused_computation.229 | loop fusion | bytes 7340040 | tf_op jit(solution)/shard_map/jit(dynamic_index_in_dim)/dynamic_slice | solution.py:202
  86.8 2.9 %copy.60 = f32[1,16,224,128]{3,2,1,0:T(8,128)} copy(f32[1,16,224,128]{2,3,1,0:T(8,128)} %get-tuple-element.27) | data formatting | bytes 3670016 | tf_op jit(solution)/shard_map/jit(dynamic_index_in_dim)/dynamic_slice | solution.py:204
  90.4 1.0 reduce_sum.70
  91.9 2.5 %collective-permute-start.16 = (f32[16,8]{0,1:T(8,128)S(1)}, f32[16,8]{0,1:T(8,128)S(1)}, u32[]{:S(2)}, u32[]{:S(2)}) collective-permute-start(f32[16,8]{0,1:T(8,128)S(1)} %dynamic-slice_bitcast_fusion.6), channel_id=1, source_target_pairs={{0,2},{2,0},{4,6},{6,4},{8,10},{10,8},{12,14},{14,12},{16,18},{18,... | collective-permute-start | bytes 1544 | tf_op jit(solution)/shard_map/ppermute | solution.py:30
  96.8 3.7 %collective-permute-start.12 = (f32[36,256]{1,0:T(8,128)S(1)}, f32[36,256]{1,0:T(8,128)S(1)}, u32[]{:S(2)}, u32[]{:S(2)}) collective-permute-start(f32[36,256]{1,0:T(8,128)S(1)} %add.383), channel_id=1, source_target_pairs={{0,6},{2,0},{4,2},{6,4},{8,14},{10,8},{12,10},{14,12},{16,22},{18,... | collective-permute-start | bytes 110600 | tf_op jit(solution)/shard_map/ppermute | solution.py:54
  101.3 1.8 %copy.59 = f32[1,16,224,128]{3,2,1,0:T(8,128)} copy(f32[1,16,224,128]{2,3,1,0:T(8,128)S(1)} %get-tuple-element.26) | data formatting | bytes 3670016 | tf_op jit(solution)/shard_map/jit(dynamic_index_in_dim)/dynamic_slice | solution.py:202
  103.1 2.2 %bitcast_add_fusion = f32[16,224,128]{2,1,0:T(8,128)S(1)} fusion(f32[16,224,128]{2,1,0:T(8,128)} %collective-permute-done.2, f32[1,16,224,128]{3,2,1,0:T(8,128)} %copy.59), kind=kLoop, calls=%fused_computation.50 | loop fusion | flops 458752 | bytes 5505024 | tf_op jit(solution)/shard_map/add | solution.py:205
  105.5 2.8 %collective-permute-start.3 = (bf16[4,224,128]{2,1,0:T(8,128)(2,1)S(1)}, bf16[4,224,128]{2,1,0:T(8,128)(2,1)S(1)}, u32[]{:S(2)}, u32[]{:S(2)}) collective-permute-start(bf16[4,224,128]{2,1,0:T(8,128)(2,1)S(1)} %get-tuple-element.28), channel_id=1, source_target_pairs={{0,2},{2,4},{4,6},{6,0},{8,10},{10,12},{12,14},{14,8},{16,18},{18,... | collective-permute-start | bytes 688136 | tf_op jit(solution)/shard_map/ppermute | solution.py:65
  108.4 1.4 %collective-permute-start.4 = (bf16[4,224,128]{2,1,0:T(8,128)(2,1)S(1)}, bf16[4,224,128]{2,1,0:T(8,128)(2,1)S(1)}, u32[]{:S(2)}, u32[]{:S(2)}) collective-permute-start(bf16[4,224,128]{2,1,0:T(8,128)(2,1)S(1)} %get-tuple-element.30), channel_id=1, source_target_pairs={{0,4},{2,6},{4,0},{6,2},{8,12},{10,14},{12,8},{14,10},{16,20},{18,... | collective-permute-start | bytes 688136 | tf_op jit(solution)/shard_map/ppermute | solution.py:65
  109.8 4.5 %collective-permute-start.15 = (f32[36,256]{1,0:T(8,128)S(1)}, f32[36,256]{1,0:T(8,128)S(1)}, u32[]{:S(2)}, u32[]{:S(2)}) collective-permute-start(f32[36,256]{1,0:T(8,128)S(1)} %add_add_fusion.1), channel_id=1, source_target_pairs={{0,24},{2,26},{4,28},{6,30},{8,0},{10,2},{12,4},{14,6},{16,8},{18,... | collective-permute-start | bytes 110600 | tf_op jit(solution)/shard_map/ppermute | solution.py:54
  115.0 1.7 %collective-permute-start.13 = (f32[36,256]{1,0:T(8,128)S(1)}, f32[36,256]{1,0:T(8,128)S(1)}, u32[]{:S(2)}, u32[]{:S(2)}) collective-permute-start(f32[36,256]{1,0:T(8,128)S(1)} %add_add_fusion.1), channel_id=1, source_target_pairs={{0,8},{2,10},{4,12},{6,14},{8,16},{10,18},{12,20},{14,22},{16,24},... | collective-permute-start | bytes 110600 | tf_op jit(solution)/shard_map/ppermute | solution.py:54
  118.4 1.7 %collective-permute-start.6 = (bf16[224,128]{1,0:T(8,128)(2,1)S(1)}, bf16[224,128]{1,0:T(8,128)(2,1)S(1)}, u32[]{:S(2)}, u32[]{:S(2)}) collective-permute-start(bf16[224,128]{1,0:T(8,128)(2,1)S(1)} %get-tuple-element.82), channel_id=1, source_target_pairs={{0,8},{2,10},{4,12},{6,14},{8,16},{10,18},{12,20},{14,22},{16,24},... | collective-permute-start | bytes 172040 | tf_op jit(solution)/shard_map/ppermute | solution.py:65
  120.0 2.2 %collective-permute-start.8 = (bf16[224,128]{1,0:T(8,128)(2,1)S(1)}, bf16[224,128]{1,0:T(8,128)(2,1)S(1)}, u32[]{:S(2)}, u32[]{:S(2)}) collective-permute-start(bf16[224,128]{1,0:T(8,128)(2,1)S(1)} %get-tuple-element.83), channel_id=1, source_target_pairs={{0,24},{2,26},{4,28},{6,30},{8,0},{10,2},{12,4},{14,6},{16,8},{18,... | collective-permute-start | bytes 172040 | tf_op jit(solution)/shard_map/ppermute | solution.py:65
  124.8 2.9 %collective-permute-done.7 = bf16[224,128]{1,0:T(8,128)(2,1)S(1)} collective-permute-done((bf16[224,128]{1,0:T(8,128)(2,1)S(1)}, bf16[224,128]{1,0:T(8,128)(2,1)S(1)}, u32[]{:S(2)}, u32[]{:S(2)}) %collective-permute-start.7) | collective-permute-done | bytes 57376 | tf_op jit(solution)/shard_map/ppermute | solution.py:65
  (129 shorter events, 43.1 us)
Async XLA Ops:
  0.6 1.5 %copy-start = (f32[1,8,16,16]{3,2,1,0:T(8,128)S(1)}, f32[1,8,16,16]{3,2,1,0:T(8,128)}, u32[]{:S(2)}) copy-start(f32[1,8,16,16]{3,2,1,0:T(8,128)} %param.18) | copy-start | bytes 24580
  0.6 8.7 %collective-permute-start = (bf16[2,8,32,128]{3,2,1,0:T(8,128)(2,1)}, bf16[2,8,32,128]{3,2,1,0:T(8,128)(2,1)S(1)}, u32[]{:S(2)}, u32[]{:S(2)}) collective-permute-start(bf16[2,8,32,128]{3,2,1,0:T(8,128)(2,1)} %bitcast.435), channel_id=1, source_target_pairs={{2,0},{4,2},{6,4},{8,6},{10,8},{12,10},{14,12},{16,14},{18,16},{20... | collective-permute-start | bytes 393224 | tf_op jit(solution)/shard_map/ppermute | solution.py:24
  10.3 1.5 %copy-start.2 = (bf16[6912,128]{1,0:T(8,128)(2,1)S(1)}, bf16[6912,128]{1,0:T(8,128)(2,1)}, u32[]{:S(2)}) copy-start(bf16[6912,128]{1,0:T(8,128)(2,1)} %param.25) | copy-start | bytes 5308420
  19.2 1.0 copy-start.3
  19.2 0.9 copy-start.6
  19.2 0.9 copy-start.7
  20.6 9.2 %collective-permute-start.1 = (bf16[2,8,32,256]{3,2,1,0:T(8,128)(2,1)S(1)}, bf16[2,8,32,256]{3,2,1,0:T(8,128)(2,1)S(1)}, u32[]{:S(2)}, u32[]{:S(2)}) collective-permute-start(bf16[2,8,32,256]{3,2,1,0:T(8,128)(2,1)S(1)} %get-tuple-element.31), channel_id=1, source_target_pairs={{0,2},{2,4},{4,6},{6,8},{8,10},{10,12},{12,14},{14,16},{16,18},{18... | collective-permute-start | bytes 786440 | tf_op jit(solution)/shard_map/ppermute | solution.py:24
  30.0 1.2 copy-start.1
  86.8 4.8 %copy-start.5 = (f32[16,256]{1,0:T(8,128)S(1)}, f32[16,256]{1,0:T(8,128)}, u32[]{:S(2)}) copy-start(f32[16,256]{1,0:T(8,128)} %param.21) | copy-start | bytes 49156
  86.8 5.0 %copy-start.4 = (f32[16,256]{1,0:T(8,128)S(1)}, f32[16,256]{1,0:T(8,128)}, u32[]{:S(2)}) copy-start(f32[16,256]{1,0:T(8,128)} %param.23) | copy-start | bytes 49156
  89.7 13.4 %collective-permute-start.2 = (f32[16,224,128]{2,1,0:T(8,128)}, f32[16,224,128]{2,1,0:T(8,128)}, u32[]{:S(2)}, u32[]{:S(2)}) collective-permute-start(f32[16,224,128]{2,1,0:T(8,128)} %bitcast.471), channel_id=1, source_target_pairs={{0,1},{1,0},{2,3},{3,2},{4,5},{5,4},{6,7},{7,6},{8,9},{9,8},{10,11... | collective-permute-start | bytes 5505032 | tf_op jit(solution)/shard_map/ppermute | solution.py:35
  91.9 4.1 %collective-permute-start.16 = (f32[16,8]{0,1:T(8,128)S(1)}, f32[16,8]{0,1:T(8,128)S(1)}, u32[]{:S(2)}, u32[]{:S(2)}) collective-permute-start(f32[16,8]{0,1:T(8,128)S(1)} %dynamic-slice_bitcast_fusion.6), channel_id=1, source_target_pairs={{0,2},{2,0},{4,6},{6,4},{8,10},{10,8},{12,14},{14,12},{16,18},{18,... | collective-permute-start | bytes 1544 | tf_op jit(solution)/shard_map/ppermute | solution.py:30
  95.6 1.3 collective-permute-start.9
  96.8 11.6 %collective-permute-start.12 = (f32[36,256]{1,0:T(8,128)S(1)}, f32[36,256]{1,0:T(8,128)S(1)}, u32[]{:S(2)}, u32[]{:S(2)}) collective-permute-start(f32[36,256]{1,0:T(8,128)S(1)} %add.383), channel_id=1, source_target_pairs={{0,6},{2,0},{4,2},{6,4},{8,14},{10,8},{12,10},{14,12},{16,22},{18,... | collective-permute-start | bytes 110600 | tf_op jit(solution)/shard_map/ppermute | solution.py:54
  100.6 9.2 %collective-permute-start.11 = (f32[36,256]{1,0:T(8,128)S(1)}, f32[36,256]{1,0:T(8,128)S(1)}, u32[]{:S(2)}, u32[]{:S(2)}) collective-permute-start(f32[36,256]{1,0:T(8,128)S(1)} %add.383), channel_id=1, source_target_pairs={{0,4},{2,6},{4,0},{6,2},{8,12},{10,14},{12,8},{14,10},{16,20},{18,... | collective-permute-start | bytes 110600 | tf_op jit(solution)/shard_map/ppermute | solution.py:54
  100.6 9.2 %collective-permute-start.10 = (f32[36,256]{1,0:T(8,128)S(1)}, f32[36,256]{1,0:T(8,128)S(1)}, u32[]{:S(2)}, u32[]{:S(2)}) collective-permute-start(f32[36,256]{1,0:T(8,128)S(1)} %add.383), channel_id=1, source_target_pairs={{0,2},{2,4},{4,6},{6,0},{8,10},{10,12},{12,14},{14,8},{16,18},{18,... | collective-permute-start | bytes 110600 | tf_op jit(solution)/shard_map/ppermute | solution.py:54
  105.5 9.5 %collective-permute-start.3 = (bf16[4,224,128]{2,1,0:T(8,128)(2,1)S(1)}, bf16[4,224,128]{2,1,0:T(8,128)(2,1)S(1)}, u32[]{:S(2)}, u32[]{:S(2)}) collective-permute-start(bf16[4,224,128]{2,1,0:T(8,128)(2,1)S(1)} %get-tuple-element.28), channel_id=1, source_target_pairs={{0,2},{2,4},{4,6},{6,0},{8,10},{10,12},{12,14},{14,8},{16,18},{18,... | collective-permute-start | bytes 688136 | tf_op jit(solution)/shard_map/ppermute | solution.py:65
  108.3 9.2 %collective-permute-start.5 = (bf16[4,224,128]{2,1,0:T(8,128)(2,1)S(1)}, bf16[4,224,128]{2,1,0:T(8,128)(2,1)S(1)}, u32[]{:S(2)}, u32[]{:S(2)}) collective-permute-start(bf16[4,224,128]{2,1,0:T(8,128)(2,1)S(1)} %get-tuple-element.29), channel_id=1, source_target_pairs={{0,6},{2,0},{4,2},{6,4},{8,14},{10,8},{12,10},{14,12},{16,22},{18,... | collective-permute-start | bytes 688136 | tf_op jit(solution)/shard_map/ppermute | solution.py:65
  108.4 9.8 %collective-permute-start.4 = (bf16[4,224,128]{2,1,0:T(8,128)(2,1)S(1)}, bf16[4,224,128]{2,1,0:T(8,128)(2,1)S(1)}, u32[]{:S(2)}, u32[]{:S(2)}) collective-permute-start(bf16[4,224,128]{2,1,0:T(8,128)(2,1)S(1)} %get-tuple-element.30), channel_id=1, source_target_pairs={{0,4},{2,6},{4,0},{6,2},{8,12},{10,14},{12,8},{14,10},{16,20},{18,... | collective-permute-start | bytes 688136 | tf_op jit(solution)/shard_map/ppermute | solution.py:65
  109.8 12.4 %collective-permute-start.15 = (f32[36,256]{1,0:T(8,128)S(1)}, f32[36,256]{1,0:T(8,128)S(1)}, u32[]{:S(2)}, u32[]{:S(2)}) collective-permute-start(f32[36,256]{1,0:T(8,128)S(1)} %add_add_fusion.1), channel_id=1, source_target_pairs={{0,24},{2,26},{4,28},{6,30},{8,0},{10,2},{12,4},{14,6},{16,8},{18,... | collective-permute-start | bytes 110600 | tf_op jit(solution)/shard_map/ppermute | solution.py:54
  114.3 8.8 %collective-permute-start.14 = (f32[36,256]{1,0:T(8,128)S(1)}, f32[36,256]{1,0:T(8,128)S(1)}, u32[]{:S(2)}, u32[]{:S(2)}) collective-permute-start(f32[36,256]{1,0:T(8,128)S(1)} %add_add_fusion.1), channel_id=1, source_target_pairs={{0,16},{2,18},{4,20},{6,22},{8,24},{10,26},{12,28},{14,30},{16,0},... | collective-permute-start | bytes 110600 | tf_op jit(solution)/shard_map/ppermute | solution.py:54
  115.0 8.1 %collective-permute-start.13 = (f32[36,256]{1,0:T(8,128)S(1)}, f32[36,256]{1,0:T(8,128)S(1)}, u32[]{:S(2)}, u32[]{:S(2)}) collective-permute-start(f32[36,256]{1,0:T(8,128)S(1)} %add_add_fusion.1), channel_id=1, source_target_pairs={{0,8},{2,10},{4,12},{6,14},{8,16},{10,18},{12,20},{14,22},{16,24},... | collective-permute-start | bytes 110600 | tf_op jit(solution)/shard_map/ppermute | solution.py:54
  118.4 6.3 %collective-permute-start.6 = (bf16[224,128]{1,0:T(8,128)(2,1)S(1)}, bf16[224,128]{1,0:T(8,128)(2,1)S(1)}, u32[]{:S(2)}, u32[]{:S(2)}) collective-permute-start(bf16[224,128]{1,0:T(8,128)(2,1)S(1)} %get-tuple-element.82), channel_id=1, source_target_pairs={{0,8},{2,10},{4,12},{6,14},{8,16},{10,18},{12,20},{14,22},{16,24},... | collective-permute-start | bytes 172040 | tf_op jit(solution)/shard_map/ppermute | solution.py:65
  120.0 4.8 %collective-permute-start.8 = (bf16[224,128]{1,0:T(8,128)(2,1)S(1)}, bf16[224,128]{1,0:T(8,128)(2,1)S(1)}, u32[]{:S(2)}, u32[]{:S(2)}) collective-permute-start(bf16[224,128]{1,0:T(8,128)(2,1)S(1)} %get-tuple-element.83), channel_id=1, source_target_pairs={{0,24},{2,26},{4,28},{6,30},{8,0},{10,2},{12,4},{14,6},{16,8},{18,... | collective-permute-start | bytes 172040 | tf_op jit(solution)/shard_map/ppermute | solution.py:65
  122.2 5.5 %collective-permute-start.7 = (bf16[224,128]{1,0:T(8,128)(2,1)S(1)}, bf16[224,128]{1,0:T(8,128)(2,1)S(1)}, u32[]{:S(2)}, u32[]{:S(2)}) collective-permute-start(bf16[224,128]{1,0:T(8,128)(2,1)S(1)} %get-tuple-element.84), channel_id=1, source_target_pairs={{0,16},{2,18},{4,20},{6,22},{8,24},{10,26},{12,28},{14,30},{16,0},... | collective-permute-start | bytes 172040 | tf_op jit(solution)/shard_map/ppermute | solution.py:65
